TPU v7x, 32 devices: a whole 2x2x4 slice. The times are simulated.
32 devices in a mesh: wide: 16 (over z, x, core), narrow: 2 (over y).
Axes of the slice: x: 2, y: 2, z: 4, core: 2. Of those that a mesh axis runs over, the one named last changes fastest.
Arguments:
- matrix_slab: float32 [16, 262144], P(None, ('wide', 'narrow')), may hold values from -6 to 6
- row_signs: int32 [262144], P(('wide', 'narrow')), may hold values from -1 to 1, as said below
- sample_rows: int32 [32768], P(('wide', 'narrow')), may hold values from 0 to 7, as said below
Outputs:
- sketch: float32 [16, 32768], P(None, ('wide', 'narrow'))
- sketch_gram: float32 [16, 16], replicated
Inputs may be any that keep to these rules, and one draw needn't show every extreme that they name: `row_signs`: each entry is +1 or -1. `sample_rows`: entry k is the offset of the k-th sampled row inside the run of 8 rows that starts at k * 8.
All inputs are finite; a program needn't handle non-finite values.
Results may differ from a plain program's by a relative error of at most 0.00013.
Values sent between devices are 32-bit elements; how exact they have to be, the bound alone decides.
No kernel may reach another device: no remote copies, remote signals or barrier semaphores. Data moves between devices by JAX's collectives and lax.ppermute only.
A program may use at most 64 MiB of HBM per device.

v0:
```python
import functools
import math

import jax
import jax.numpy as jnp
from jax import lax
from jax.experimental import pallas as pl
from jax.experimental.pallas import tpu as pltpu
from jax.sharding import PartitionSpec as P

LANES = 128
SUBLANES = 8
AXES = ("wide", "narrow")
BIT_AXES = ("bit3", "bit2", "bit1", "bit0", "narrow")
FIRST_ORDER = ("bit1", "bit0", "narrow", "bit2", "bit3")
SECOND_ORDER = ("bit1", "bit0", "narrow", "bit2", "bit3")
VMEM_LIMIT = 32 * 1024 * 1024
MESSAGE_ROWS = 6


def positions(order, other):
    count = 2 ** len(order)
    found = []
    for place in range(count):
        bits = {axis: place >> (len(order) - 1 - rank) & 1 for rank, axis in enumerate(order)}
        found.append(sum(bits[axis] << (len(other) - 1 - rank) for rank, axis in enumerate(other)))
    return tuple(found)


def butterfly(values):
    values = list(values)
    apart = 1
    while apart < len(values):
        for low in range(len(values)):
            if not low & apart:
                first, second = values[low], values[low | apart]
                values[low], values[low | apart] = first + second, first - second
        apart *= 2
    return values


def sylvester(order_size):
    rows = lax.broadcasted_iota(jnp.int32, (order_size, order_size), 0)
    cols = lax.broadcasted_iota(jnp.int32, (order_size, order_size), 1)
    common = rows & cols
    parity = jnp.zeros_like(common)
    for bit_pos in range(order_size.bit_length() - 1):
        parity = parity ^ (common >> bit_pos)
    return (1 - 2 * (parity & 1)).astype(jnp.float32)


def split_dot(values, table, parts=3):
    total = None
    for _ in range(parts):
        part = values.astype(jnp.bfloat16)
        values = values - part.astype(jnp.float32)
        product = jnp.dot(part, table, preferred_element_type=jnp.float32)
        total = product if total is None else total + product
    return total


def butterfly_steps(count):
    steps = []
    apart = 1
    while apart < count:
        radix = min(8, count // apart)
        for start in range(count):
            if start // apart % radix == 0:
                steps.append((apart, [start + apart * index for index in range(radix)]))
        apart *= radix
    return steps


def fetch_blocks(x_hbm, signs_hbm, out_ref, x_ref, signs_ref, arrived):
    blocks, columns, _ = out_ref.shape
    fetches = [pltpu.make_async_copy(signs_hbm, signs_ref, arrived.at[0])]
    places = [pl.ds(start, SUBLANES) for start in range(0, columns, SUBLANES)]
    for index, place in enumerate(places):
        fetches.append(
            pltpu.make_async_copy(x_hbm.at[place], x_ref.at[place], arrived.at[index + 1])
        )
    for fetch in fetches:
        fetch.start()
    table = sylvester(LANES).astype(jnp.bfloat16)
    fetches[0].wait()
    for index, place in enumerate(places):
        fetches[index + 1].wait()
        signed = []
        for block in range(blocks):
            signs = signs_ref[block : block + 1, :].astype(jnp.float32)
            signed.append(x_ref[place, block * LANES : (block + 1) * LANES] * signs)
        mixed = split_dot(jnp.concatenate(signed, axis=0), table)
        out_ref[:, place, :] = mixed.reshape(blocks, SUBLANES, LANES)


def local_kernel(x_hbm, signs_hbm, out_ref, x_ref, signs_ref, arrived):
    fetch_blocks(x_hbm, signs_hbm, out_ref, x_ref, signs_ref, arrived)
    for apart, places in butterfly_steps(out_ref.shape[0]):
        for place, value in zip(places, butterfly([out_ref[p] for p in places])):
            out_ref[place] = value


def sliced_kernel(
    x_hbm, signs_hbm, samples_hbm, final_ref, out_ref, x_ref, signs_ref, samples_ref, arrived, noted
):
    note = pltpu.make_async_copy(samples_hbm, samples_ref, noted)
    note.start()
    fetch_blocks(x_hbm, signs_hbm, out_ref, x_ref, signs_ref, arrived)
    blocks, columns, _ = out_ref.shape
    slices = blocks // 2
    rows = final_ref.shape[0] // slices
    note.wait()
    samples = samples_ref[...].astype(jnp.float32)
    per_row = slices // samples.shape[0]
    for turn in range(per_row):
        shift = LANES - turn * LANES // per_row
        turned = pltpu.roll(samples, shift, 1) if turn else samples
        for index in range(turn, slices, per_row):
            tail = (index + 1) * rows - 1
            final_ref[tail : tail + 1, :] = turned[index // per_row : index // per_row + 1]
    steps = butterfly_steps(blocks)
    last = steps[-1][0]
    for apart, places in steps:
        for place, value in zip(places, butterfly([out_ref[p] for p in places])):
            if apart == last:
                start = place // 2 * rows + place % 2 * columns
                final_ref[start : start + columns, :] = value
            else:
                out_ref[place] = value


def in_vmem(count):
    return [pl.BlockSpec(memory_space=pltpu.VMEM)] * count


def in_hbm(*arrays):
    return [pltpu.with_memory_space_constraint(array, pltpu.HBM) for array in arrays]


def fetch_scratch(matrix_slab, blocks):
    return [
        pltpu.VMEM(matrix_slab.shape, jnp.float32),
        pltpu.VMEM((blocks, LANES), jnp.int32),
    ]


def local_transform(matrix_slab, row_signs):
    columns, row_count = matrix_slab.shape
    blocks = row_count // LANES
    return pl.pallas_call(
        local_kernel,
        out_shape=jax.ShapeDtypeStruct((blocks, columns, LANES), jnp.float32),
        in_specs=[pl.BlockSpec(memory_space=pltpu.HBM)] * 2,
        out_specs=in_vmem(1)[0],
        scratch_shapes=[
            *fetch_scratch(matrix_slab, blocks),
            pltpu.SemaphoreType.DMA((columns // SUBLANES + 1,)),
        ],
        compiler_params=pltpu.CompilerParams(vmem_limit_bytes=VMEM_LIMIT),
    )(*in_hbm(matrix_slab, row_signs.reshape(blocks, LANES)))


def sliced_transform(matrix_slab, row_signs, sample_rows):
    columns, row_count = matrix_slab.shape
    blocks = row_count // LANES
    samples = sample_rows.reshape(-1, LANES)
    return pl.pallas_call(
        sliced_kernel,
        out_shape=jax.ShapeDtypeStruct((blocks // 2 * (2 * columns + 1), LANES), jnp.float32),
        in_specs=[pl.BlockSpec(memory_space=pltpu.HBM)] * 3,
        out_specs=in_vmem(1)[0],
        scratch_shapes=[
            pltpu.VMEM((blocks, columns, LANES), jnp.float32),
            *fetch_scratch(matrix_slab, blocks),
            pltpu.VMEM(samples.shape, jnp.int32),
            pltpu.SemaphoreType.DMA((columns // SUBLANES + 1,)),
            pltpu.SemaphoreType.DMA(()),
        ],
        compiler_params=pltpu.CompilerParams(vmem_limit_bytes=VMEM_LIMIT),
    )(*in_hbm(matrix_slab, row_signs.reshape(blocks, LANES), samples))


def mix_kernel(run_length, scale, gram_scale, places, x_ref, out_ref):
    devices = out_ref.shape[0] // MESSAGE_ROWS
    rows = x_ref.shape[0] // devices
    runs = LANES // run_length
    samples = jnp.concatenate(
        [x_ref[(s + 1) * rows - 1 : (s + 1) * rows, :] for s in range(devices)], axis=0
    ).astype(jnp.bfloat16)
    run_of = lax.broadcasted_iota(jnp.int32, (LANES, 2 * LANES), 0)
    row_of = lax.broadcasted_iota(jnp.int32, (LANES, 2 * LANES), 1)
    spread = jnp.where(row_of // run_length == run_of, 1.0, 0.0).astype(jnp.bfloat16)
    offsets = jnp.dot(samples, spread, preferred_element_type=jnp.float32)
    own = lax.broadcasted_iota(jnp.int32, offsets.shape, 1) % run_length
    mask = jnp.where(offsets == own.astype(jnp.float32), scale, 0.0)
    picked = []
    for part in range(4):
        block = part // 2
        starts = [s * rows + part * SUBLANES for s in range(devices)]
        mixed = butterfly([x_ref[start : start + SUBLANES, :] for start in starts])
        picked.append(
            jnp.concatenate(
                [
                    mixed[d] * mask[d : d + 1, block * LANES : (block + 1) * LANES]
                    for d in range(devices)
                ],
                axis=0,
            )
        )
    quarter = 2 * runs
    row = lax.broadcasted_iota(jnp.int32, (LANES, LANES), 0)
    lane = lax.broadcasted_iota(jnp.int32, (LANES, LANES), 1)
    pattern = jnp.where(row // run_length == lane % runs, 1.0, 0.0)
    lane = lax.broadcasted_iota(jnp.int32, (1, LANES), 1)
    group = lane // quarter
    place = []
    for part in range(4):
        block, half = part // 2, part % 2
        here = lane // runs % 2 == block
        sides = [group % 2, jnp.where(group < 2, group, 3 - group)]
        masks = [jnp.where(here & (side == half), 1.0, 0.0) for side in sides]
        place.append(jnp.concatenate([(pattern * mask).astype(jnp.bfloat16) for mask in masks], axis=1))
    gathered = split_dot(jnp.concatenate(picked, axis=1), jnp.concatenate(place, axis=0), 2)
    straight, crossed = gathered[:, :LANES], gathered[:, LANES:]
    turns = SUBLANES // 2 + 1
    totals = []
    for turn in range(turns):
        total = None
        for d in range(devices):
            one = straight[d * SUBLANES : (d + 1) * SUBLANES]
            two = crossed[d * SUBLANES : (d + 1) * SUBLANES]
            if turn:
                two = pltpu.roll(two, SUBLANES - turn, 0)
            total = one * two if total is None else total + one * two
        totals.append(total)
    from_quarter = row // quarter
    together = [jnp.where(from_quarter == q, 1.0, 0.0).astype(jnp.bfloat16) for q in range(4)]
    sums = split_dot(jnp.concatenate(totals, axis=0), jnp.concatenate(together, axis=1)) * gram_scale
    sub = lax.broadcasted_iota(jnp.int32, (SUBLANES, LANES), 0)
    lane = lax.broadcasted_iota(jnp.int32, (SUBLANES, LANES), 1)
    first, second = [jnp.zeros((SUBLANES, LANES), jnp.float32)] * 2
    for turn in range(SUBLANES):
        known = min(turn, SUBLANES - turn)
        here = sums[known * SUBLANES : (known + 1) * SUBLANES]
        quarters = [here[:, q * LANES : (q + 1) * LANES] for q in range(4)]
        if known != turn:
            quarters = [pltpu.roll(quarters[q], known, 0) for q in (0, 1, 3, 2)]
        mine = lane % SUBLANES == (sub + turn) % SUBLANES
        left = lane // SUBLANES % 2 == 0
        first = jnp.where(mine, jnp.where(left, quarters[0], quarters[2]), first)
        second = jnp.where(mine, jnp.where(left, quarters[3], quarters[1]), second)
    in_place = lane // (2 * SUBLANES) == sub
    gram = jnp.concatenate(
        [jnp.sum(jnp.where(in_place, part, 0.0), axis=0, keepdims=True) for part in (first, second)],
        axis=0,
    )
    half = SUBLANES // 2
    lane = lax.broadcasted_iota(jnp.int32, (half, LANES), 1)
    for d in range(devices):
        one = straight[d * SUBLANES : (d + 1) * SUBLANES]
        start = places[d] * MESSAGE_ROWS
        out_ref[start : start + half, :] = jnp.where(lane < LANES // 2, one[:half], one[half:])
        out_ref[start + half : start + MESSAGE_ROWS, :] = gram


def mix_and_pick(received, devices, run_length, scale, gram_scale, places):
    return pl.pallas_call(
        functools.partial(mix_kernel, run_length, scale, gram_scale, places),
        out_shape=jax.ShapeDtypeStruct((devices * MESSAGE_ROWS, LANES), jnp.float32),
        in_specs=in_vmem(1),
        out_specs=in_vmem(1)[0],
        compiler_params=pltpu.CompilerParams(vmem_limit_bytes=VMEM_LIMIT),
    )(received)


def finish_kernel(places, x_ref, sketch_ref, gram_ref):
    sources = x_ref.shape[0] // MESSAGE_ROWS
    quarter = LANES // 4
    half_rows = SUBLANES // 2
    sub = lax.broadcasted_iota(jnp.int32, (SUBLANES, LANES), 0)
    lane = lax.broadcasted_iota(jnp.int32, (SUBLANES, LANES), 1)
    gram = None
    for start in range(0, sources, 4):
        halves = [None, None]
        for index in range(4):
            place = places[start + index] * MESSAGE_ROWS
            tail = x_ref[place + half_rows : place + MESSAGE_ROWS, :]
            gram = tail if gram is None else gram + tail
            piece = x_ref[place : place + half_rows, :]
            piece = jnp.concatenate([piece, piece], axis=0)
            piece = jnp.where(sub < half_rows, piece, pltpu.roll(piece, LANES // 2, 1))
            for half in range(2):
                shift = (index - half) % 4 * quarter
                moved = pltpu.roll(piece, shift, 1) if shift else piece
                if halves[half] is None:
                    halves[half] = moved
                else:
                    halves[half] = jnp.where(lane // quarter == index, moved, halves[half])
        for half in range(2):
            sketch_ref[
                half * SUBLANES : (half + 1) * SUBLANES, start * quarter : (start + 4) * quarter
            ] = halves[half]
    columns = gram_ref.shape[0]
    for half in range(2):
        for row in range(SUBLANES):
            line = gram[half : half + 1]
            line = pltpu.roll(line, LANES - row * columns, 1) if row else line
            gram_ref[half * SUBLANES + row : half * SUBLANES + row + 1, :] = line[:, :columns]


def finish(received, columns, sample_count, places):
    return pl.pallas_call(
        functools.partial(finish_kernel, places),
        out_shape=(
            jax.ShapeDtypeStruct((columns, sample_count), jnp.float32),
            jax.ShapeDtypeStruct((columns, columns), jnp.float32),
        ),
        in_specs=[pl.BlockSpec(memory_space=pltpu.VMEM)],
        out_specs=(pl.BlockSpec(memory_space=pltpu.VMEM),) * 2,
        compiler_params=pltpu.CompilerParams(vmem_limit_bytes=VMEM_LIMIT),
    )(received)


def exchange(values, axes):
    return lax.all_to_all(values, axes, split_axis=0, concat_axis=0, tiled=True)


def general_shards(matrix_slab, row_signs, sample_rows):
    columns, row_count = matrix_slab.shape
    sample_count = sample_rows.shape[0]
    devices = lax.axis_size("wide") * lax.axis_size("narrow")
    run_length = row_count // sample_count
    slice_rows = row_count // devices
    slice_runs = slice_rows // run_length
    values = jnp.swapaxes(local_transform(matrix_slab, row_signs), 0, 1)
    values = values.reshape(columns, devices, slice_rows)
    received = exchange(jnp.swapaxes(values, 0, 1), AXES)
    offsets = exchange(sample_rows.reshape(devices, slice_runs), AXES)
    mixed = jnp.einsum("ds,scr->dcr", sylvester(devices), received, precision=lax.Precision.HIGHEST)
    mixed = mixed.reshape(devices, columns, slice_runs, run_length)
    chosen = offsets[:, None, :, None] == lax.iota(jnp.int32, run_length)
    picked = jnp.sum(jnp.where(chosen, mixed, 0.0), axis=3)
    picked = picked * jnp.float32(1.0 / math.sqrt(row_count * devices))
    gram = jnp.einsum("dck,dek->ce", picked, picked, precision=lax.Precision.HIGHEST)
    gram = gram / jnp.float32(sample_count * devices)
    grams = jnp.broadcast_to(gram[None], (devices, columns, columns))
    back = exchange(jnp.concatenate([picked, grams], axis=2), AXES)
    sketch = jnp.swapaxes(back[:, :, :slice_runs], 0, 1).reshape(columns, devices * slice_runs)
    return sketch, jnp.sum(back[:, :, slice_runs:], axis=0)


def sliced_shards(matrix_slab, row_signs, sample_rows):
    columns, row_count = matrix_slab.shape
    sample_count = sample_rows.shape[0]
    devices = lax.axis_size(FIRST_ORDER)
    places = positions(FIRST_ORDER, SECOND_ORDER)
    run_length = row_count // sample_count
    sent = sliced_transform(matrix_slab, row_signs, sample_rows)
    received = exchange(sent.reshape(devices, -1), FIRST_ORDER).reshape(sent.shape)
    scale = 1.0 / math.sqrt(row_count * devices)
    gram_scale = 1.0 / (sample_count * devices)
    picked = mix_and_pick(received, devices, run_length, scale, gram_scale, places)
    returned = exchange(picked.reshape(devices, -1), SECOND_ORDER).reshape(picked.shape)
    return finish(returned, columns, sample_count, places)


def solution(mesh):
    axes, function = AXES, general_shards
    if (mesh.shape["wide"], mesh.shape["narrow"]) == (16, 2):
        axes, function = BIT_AXES, sliced_shards
        mesh = jax.sharding.Mesh(mesh.devices.reshape((2,) * len(axes)), axes)
    in_specs = (P(None, axes), P(axes), P(axes))
    out_specs = (P(None, axes), P())
    return jax.shard_map(function, mesh=mesh, in_specs=in_specs, out_specs=out_specs, check_vma=False)
```

profile of v0, /device:TPU:0, one launch (start us, length us, event | category | flops | bytes accessed | tf_op | source)
XLA Modules:
  0.0 37.3 jit_solution(17030988163478631144)
XLA Ops:
  0.6 1.8 %shard_map.50 = f32[1056,128]{1,0:T(8,128)S(1)} custom-call(f32[16,8192]{1,0:T(8,128)} %x_hbm.1, s32[64,128]{1,0:T(8,128)} %bitcast.10, s32[8,128]{1,0:T(8,128)} %bitcast.11), custom_call_target="tpu_custom_call" | custom-call | tf_op jit(solution)/shard_map/pallas_call | solution.py:167
  2.4 23.8 %all_to_all.18 = f32[32,1,4224]{2,1,0:T(1,128)S(1)} all-to-all(f32[32,1,4224]{2,1,0:T(1,128)S(1)} %bitcast.7), channel_id=1, replica_groups=mesh['bit3'=2,'bit2'=2,'bit1'=2,'bit0'=2,'narrow'=2] {'bit1','bit0','nar..., dimensions={0} | all-to-all | bytes 1081344 | tf_op jit(solution)/shard_map/all_to_all | solution.py:325
  26.2 0.7 %shard_map.51 = f32[192,128]{1,0:T(8,128)S(1)} custom-call(f32[1056,128]{1,0:T(8,128)S(1)} %bitcast.6), custom_call_target="tpu_custom_call" | custom-call | tf_op jit(solution)/shard_map/pallas_call | solution.py:267
  27.0 9.4 %all_to_all.19 = f32[32,1,768]{2,1,0:T(1,128)S(1)} all-to-all(f32[32,1,768]{2,1,0:T(1,128)S(1)} %bitcast.9), channel_id=1, replica_groups=mesh['bit3'=2,'bit2'=2,'bit1'=2,'bit0'=2,'narrow'=2] {'bit1','bit0','nar..., dimensions={0} | all-to-all | bytes 196608 | tf_op jit(solution)/shard_map/all_to_all | solution.py:325
  36.4 0.8 %shard_map.52 = (f32[16,1024]{1,0:T(8,128)}, f32[16,16]{1,0:T(8,128)}) custom-call(f32[192,128]{1,0:T(8,128)S(1)} %bitcast.8), custom_call_target="tpu_custom_call" | custom-call | tf_op jit(solution)/shard_map/pallas_call | solution.py:312
where the time goes:
time: 37.4 us; the launch traced here: 37.3 us
  blocking collectives  33.3 us (89%)
  Pallas kernels  3.37 us (9%)
  between operations  0.65 us (2%)
    all_to_all x2, blocking collectives, exchange(): return lax.all_to_all(values, axes, split_axis=0, concat_axis=0, tiled=True)  33.3 us
    pallas_call x1, Pallas kernels, sliced_transform(): pl.pallas_call(sliced_kernel, out_shape=jax.ShapeDtypeStruct((blocks // 2...  1.79 us
    pallas_call x1, Pallas kernels, finish(): pl.pallas_call(functools.partial(finish_kernel, places), out_shape=(jax.S...  0.83 us

commit v1 on v0

--- a/solution.py
+++ b/solution.py
@@ -12,8 +12,8 @@
 SUBLANES = 8
 AXES = ("wide", "narrow")
 BIT_AXES = ("bit3", "bit2", "bit1", "bit0", "narrow")
-FIRST_ORDER = ("bit1", "bit0", "narrow", "bit2", "bit3")
-SECOND_ORDER = ("bit1", "bit0", "narrow", "bit2", "bit3")
+FIRST_ORDER = ("bit0", "bit1", "narrow", "bit3", "bit2")
+SECOND_ORDER = ("bit0", "bit1", "narrow", "bit3", "bit2")
 VMEM_LIMIT = 32 * 1024 * 1024
 MESSAGE_ROWS = 6
 

time: 37.4 us -> 37.6 us (level)
  no operation moved by 1% of the time
where the time goes in v1:
time: 37.6 us; the launch traced here: 37.4 us
  blocking collectives  33.4 us (89%)
  Pallas kernels  3.37 us (9%)
  between operations  0.65 us (2%)
    all_to_all x2, blocking collectives, exchange(): return lax.all_to_all(values, axes, split_axis=0, concat_axis=0, tiled=True)  33.4 us
    pallas_call x1, Pallas kernels, sliced_transform(): pl.pallas_call(sliced_kernel, out_shape=jax.ShapeDtypeStruct((blocks // 2...  1.79 us
    pallas_call x1, Pallas kernels, finish(): pl.pallas_call(functools.partial(finish_kernel, places), out_shape=(jax.S...  0.83 us

profile of v1, /device:TPU:0, one launch (start us, length us, event | category | flops | bytes accessed | tf_op | source)
XLA Modules:
  0.0 37.4 jit_solution(10051742947059686543)
XLA Ops:
  0.6 1.8 %shard_map.50 = f32[1056,128]{1,0:T(8,128)S(1)} custom-call(f32[16,8192]{1,0:T(8,128)} %x_hbm.1, s32[64,128]{1,0:T(8,128)} %bitcast.10, s32[8,128]{1,0:T(8,128)} %bitcast.11), custom_call_target="tpu_custom_call" | custom-call | tf_op jit(solution)/shard_map/pallas_call | solution.py:167
  2.4 23.7 %all_to_all.18 = f32[32,1,4224]{2,1,0:T(1,128)S(1)} all-to-all(f32[32,1,4224]{2,1,0:T(1,128)S(1)} %bitcast.7), channel_id=1, replica_groups=mesh['bit3'=2,'bit2'=2,'bit1'=2,'bit0'=2,'narrow'=2] {'bit0','bit1','nar..., dimensions={0} | all-to-all | bytes 1081344 | tf_op jit(solution)/shard_map/all_to_all | solution.py:325
  26.1 0.7 %shard_map.51 = f32[192,128]{1,0:T(8,128)S(1)} custom-call(f32[1056,128]{1,0:T(8,128)S(1)} %bitcast.6), custom_call_target="tpu_custom_call" | custom-call | tf_op jit(solution)/shard_map/pallas_call | solution.py:267
  26.9 9.7 %all_to_all.19 = f32[32,1,768]{2,1,0:T(1,128)S(1)} all-to-all(f32[32,1,768]{2,1,0:T(1,128)S(1)} %bitcast.9), channel_id=1, replica_groups=mesh['bit3'=2,'bit2'=2,'bit1'=2,'bit0'=2,'narrow'=2] {'bit0','bit1','nar..., dimensions={0} | all-to-all | bytes 196608 | tf_op jit(solution)/shard_map/all_to_all | solution.py:325
  36.6 0.8 %shard_map.52 = (f32[16,1024]{1,0:T(8,128)}, f32[16,16]{1,0:T(8,128)}) custom-call(f32[192,128]{1,0:T(8,128)S(1)} %bitcast.8), custom_call_target="tpu_custom_call" | custom-call | tf_op jit(solution)/shard_map/pallas_call | solution.py:312
